TPU v7x, 32 devices: a whole 2x2x4 slice. The times are simulated.
32 devices in a mesh: face: 2 (over core), elem: 16 (over z, y, x).
Axes of the slice: x: 2, y: 2, z: 4, core: 2. Of those that a mesh axis runs over, the one named last changes fastest.
Arguments:
- state: float32 [432, 32, 2048], P(None, 'face', 'elem'), may hold values from -6 to 6
- speed_x: float32 [432], replicated, may hold values from -0.25 to 0.25
- speed_y: float32 [432], replicated, may hold values from -0.25 to 0.25
- w_in: bfloat16 [512, 432], replicated, may hold values from -0.3125 to 0.3125
- b_in: float32 [512], replicated, may hold values from -1.8 to 1.8
- w_mid: bfloat16 [512, 512], replicated, may hold values from -0.25 to 0.25
- b_mid: float32 [512], replicated, may hold values from -1.8 to 1.8
- w_top: bfloat16 [512, 512], replicated, may hold values from -0.25 to 0.25
- b_top: float32 [512], replicated, may hold values from -1.8 to 1.8
- w_out: bfloat16 [360, 512], replicated, may hold values from -0.25 to 0.25
- b_out: float32 [360], replicated, may hold values from -1.8 to 1.8
- span_of: int32 [2, 16, 2048, 1], P('face', 'elem'), may hold values from 0 to 31; in each aligned block of 2048 rows (0 to 2047, 2048 to 4095, ..., all dimensions but the last counted through in order) at most 128 rows name the same one
Outputs:
- final_state: float32 [432, 32, 2048], P(None, 'face', 'elem')
- tendencies: bfloat16 [360, 32, 2048], P(None, 'face', 'elem')
- span_heating: float32 [32], P(('face', 'elem'))
Inputs may be any that keep to these rules, and one draw needn't show every extreme that they name: `span_of`: among the columns of one device, no span is named more than 128 times, a bound that some block reaches; every span is named by some column.
All inputs are finite; a program needn't handle non-finite values.
Results may differ from a plain program's by a relative error of at most 0.0095.
Values may be sent and summed in bfloat16 or wider, within the bound.
A program may use at most 128 MiB of HBM per device.

v0:
```python
import functools
import math

import jax
import jax.numpy as jnp
import numpy as np
from jax import lax
from jax.experimental import pallas as pl
from jax.experimental.pallas import tpu as pltpu
from jax.sharding import PartitionSpec as P

NP = 4
LEV = 72
CHUNKS = 3
MESH = pl.DeviceIdType.MESH
SX_SLOT = (0, 1, 6, 7)
SY_SLOT = (2, 3, 4, 5)


def gll_matrix():
    inner_node = 1.0 / math.sqrt(5.0)
    nodes = np.array([-1.0, -inner_node, inner_node, 1.0])
    weights = np.array(
        [1.0 / np.prod([nodes[j] - nodes[k] for k in range(4) if k != j]) for j in range(4)]
    )
    matrix = np.zeros((4, 4))
    for i in range(4):
        for j in range(4):
            if i != j:
                matrix[i, j] = weights[j] / weights[i] / (nodes[i] - nodes[j])
    for i in range(4):
        matrix[i, i] = -np.sum(matrix[i])
    return matrix


def operator_tables(breadth):
    table = gll_matrix()
    deriv = np.kron(np.eye(breadth // NP), table)
    avg = np.eye(breadth)
    for j in range(breadth):
        if j % NP == NP - 1:
            avg[j, j] = 0.5
            if j + 1 < breadth:
                avg[j, j + 1] = 0.5
        elif j % NP == 0:
            avg[j, j] = 0.5
            if j > 0:
                avg[j, j - 1] = 0.5
    across = (avg @ deriv).T
    half = (0.5, 1.0, 1.0, 0.5)
    tables = []
    for pair, slots in enumerate(((0, 1, 2, 3, 4, 5), (2, 3, 4, 5, 6, 7))):
        out = np.zeros((6 * breadth, 2 * breadth))
        for col in range(2):
            j = 2 * pair + col
            for at, slot in enumerate(slots):
                if slot == SX_SLOT[j]:
                    block = half[j] * across
                elif slot in SY_SLOT:
                    block = half[j] * table[j, SY_SLOT.index(slot)] * avg.T
                else:
                    continue
                out[at * breadth : (at + 1) * breadth, col * breadth : (col + 1) * breadth] = block
        tables.append(out)
    return np.stack(tables).astype(np.float32)


def edge_tables(breadth):
    pick = np.zeros((NP * breadth, 2 * breadth), np.float32)
    place = np.zeros((breadth, NP * breadth), np.float32)
    for lane in range(breadth):
        j, side = divmod(lane % (2 * NP), 2)
        edge = 0 if side else breadth - 1
        pick[j * breadth + edge, lane] = 1.0
        pick[(NP - 1 - j) * breadth + edge, breadth + lane] = 1.0
        place[lane, j * breadth + (breadth - 1 if side else 0)] = 1.0
    return pick, place


def advect_kernel(
    n_face,
    n_elem,
    height,
    breadth,
    state_hbm,
    speed_ref,
    table_ref,
    pick_ref,
    place_ref,
    final_hbm,
    inputs_ref,
    field,
    base,
    slots,
    raw,
    rows16,
    edged,
    x_send,
    x_recv,
    y_send,
    y_recv,
    load_sem,
    store_sem,
    send_sem,
    recv_sem,
):
    feats = speed_ref.shape[0]
    size = feats // CHUNKS
    rows = size * height
    elements = height // NP
    face, elem = lax.axis_index("face"), lax.axis_index("elem")
    other = lax.rem(face + 1, n_face)
    right, left = lax.rem(elem + 1, n_elem), lax.rem(elem + n_elem - 1, n_elem)
    partners = ((face, left), (face, right), (other, left), (other, right), (other, elem))

    def load(chunk):
        at = pl.ds(chunk * rows, rows)
        return pltpu.make_async_copy(state_hbm.at[at], field.at[at], load_sem.at[chunk])

    def store(chunk):
        at = pl.ds(chunk * rows, rows)
        return pltpu.make_async_copy(field.at[at], final_hbm.at[at], store_sem.at[chunk])

    for chunk in range(CHUNKS):
        load(chunk).start()

    barrier = pltpu.get_barrier_semaphore()
    for partner in partners:
        pl.semaphore_signal(barrier, inc=1, device_id=partner, device_id_type=MESH)
    pl.semaphore_wait(barrier, len(partners))

    def copies(step):
        made = []
        for at in range(4):
            made.append(
                pltpu.make_async_remote_copy(
                    src_ref=x_send.at[step, at // 2],
                    dst_ref=x_recv.at[step, at],
                    send_sem=send_sem.at[step, at],
                    recv_sem=recv_sem.at[step, at],
                    device_id=partners[at],
                    device_id_type=MESH,
                )
            )
        made.append(
            pltpu.make_async_remote_copy(
                src_ref=y_send.at[step],
                dst_ref=y_recv.at[step],
                send_sem=send_sem.at[step, 4],
                recv_sem=recv_sem.at[step, 4],
                device_id=partners[4],
                device_id_type=MESH,
            )
        )
        return made

    lane = lax.broadcasted_iota(jnp.int32, (16, breadth), 1)
    groups = 3
    trips = size // (16 * groups)

    def speeds(chunk, at):
        pair = speed_ref[pl.ds(pl.multiple_of(chunk * size + at, 16), 16), :]
        across = jnp.broadcast_to(-pair[:, 0:1], (16, breadth))
        down = jnp.broadcast_to(-pair[:, 1:2], (16, breadth))
        return across, down

    def put_slots(at, y, value, across, down):
        element, j = divmod(y, NP)
        place = pl.ds(pl.multiple_of(element * size + at, 16), 16)
        sx, sy = SX_SLOT[j] * breadth, SY_SLOT[j] * breadth
        slots[place, sx : sx + breadth] = (across * value).astype(jnp.bfloat16)
        slots[place, sy : sy + breadth] = (down * value).astype(jnp.bfloat16)

    def field_at(chunk, at, y):
        return pl.ds((chunk * size + at) * height + y, 16, stride=height)

    def raw_at(chunk, at, y):
        element, j = divmod(y, NP)
        place = pl.ds(pl.multiple_of(element * size + at, 16), 16)
        return raw[chunk, j // 2, place, (j % 2) * breadth : (j % 2 + 1) * breadth]

    def prepare(chunk):
        @pl.loop(0, size // 16)
        def _(block):
            at = block * 16
            across, down = speeds(chunk, at)
            for y in range(height):
                put_slots(at, y, field[field_at(chunk, at, y), :], across, down)

    def apply_and_send(stage, chunk):
        step = stage * CHUNKS + chunk
        for pair in range(2):
            raw[chunk, pair] = jnp.dot(
                slots[:, 2 * pair * breadth : (2 * pair + 6) * breadth],
                table_ref[pair],
                preferred_element_type=jnp.float32,
            )
        y_send[step, 0] = raw[chunk, 0, 0:size, 0:breadth].astype(jnp.bfloat16)
        y_send[step, 1] = raw[
            chunk, 1, (elements - 1) * size : elements * size, breadth : 2 * breadth
        ].astype(jnp.bfloat16)

        for pair in range(2):
            rows16[:, 2 * pair * breadth : 2 * (pair + 1) * breadth] = raw[chunk, pair].astype(
                jnp.bfloat16
            )
        edged[:, 0 : 2 * breadth] = jnp.dot(
            rows16[...], pick_ref[...], preferred_element_type=jnp.float32
        )

        @pl.loop(0, trips)
        def _(trip):
            for kind in range(2):
                packed = jnp.zeros((16, breadth), jnp.float32)
                for group in range(groups):
                    at = (trip * groups + group) * 16
                    for element in range(elements):
                        there = edged[
                            pl.ds(pl.multiple_of(element * size + at, 16), 16),
                            kind * breadth : (kind + 1) * breadth,
                        ]
                        spot = elements - 1 - element if kind else element
                        packed = jnp.where(
                            lane // (2 * NP) == elements * group + spot, there, packed
                        )
                x_send[step, kind, pl.ds(pl.multiple_of(trip * 16, 16), 16), :] = packed.astype(
                    jnp.bfloat16
                )

        for copy in copies(step):
            copy.start()

    def finish(stage, chunk):
        step = stage * CHUNKS + chunk
        for copy in copies(step):
            copy.wait_recv()

        @pl.loop(0, trips)
        def _(trip):
            packed_at = pl.ds(pl.multiple_of(trip * 16, 16), 16)

            def merged(first):
                from_right = x_recv[step, first, packed_at, :].astype(jnp.float32)
                from_left = x_recv[step, first + 1, packed_at, :].astype(jnp.float32)
                return jnp.where(lane % 2 == 0, from_left, from_right)

            y_of = lane // 2 % height
            outer = (y_of == 0) | (y_of == height - 1)
            total = merged(0) + jnp.where(outer, merged(2), 0.0)
            for group in range(groups):
                at = (trip * groups + group) * 16
                for element in range(elements):
                    own_lanes = lane // (2 * NP) == elements * group + element
                    rows16[pl.ds(pl.multiple_of(element * size + at, 16), 16), 0:breadth] = (
                        jnp.where(own_lanes, total, 0.0).astype(jnp.bfloat16)
                    )

        edged[...] = jnp.dot(
            rows16[:, 0:breadth], place_ref[...], preferred_element_type=jnp.float32
        )

        @pl.loop(0, trips)
        def _(trip):
            for group in range(groups):
                at = (trip * groups + group) * 16

                def own(y):
                    element, j = divmod(y, NP)
                    added = edged[
                        pl.ds(pl.multiple_of(element * size + at, 16), 16),
                        j * breadth : (j + 1) * breadth,
                    ]
                    return raw_at(chunk, at, y) + added

                def across_face(row):
                    there = y_recv[step, row, pl.ds(pl.multiple_of(at, 16), 16), :]
                    return there.astype(jnp.float32)

                across, down = speeds(chunk, at)

                def update(y, tendency):
                    kept = pl.ds(pl.multiple_of(chunk * size + at, 16), 16)
                    if stage == 0:
                        first = field[field_at(chunk, at, y), :]
                        base[y, kept, :] = first + 0.25 * tendency
                        value = first + tendency
                    elif stage == 1:
                        first = field[field_at(chunk, at, y), :]
                        value = base[y, kept, :] + 0.25 * tendency
                        base[y, kept, :] = first * (1.0 / 3.0) + value * (2.0 / 3.0)
                    else:
                        value = base[y, kept, :] + (2.0 / 3.0) * tendency
                        field[field_at(chunk, at, y), :] = value
                        half = (y % 2) * breadth
                        inputs_ref[y // 2, kept, half : half + breadth] = value.astype(
                            jnp.bfloat16
                        )
                        return
                    put_slots(at, y, value, across, down)

                for y in range(height):
                    if y == 0:
                        update(y, own(y) + across_face(1))
                    elif y == height - 1:
                        update(y, own(y) + across_face(0))
                    elif y % NP == NP - 1:
                        both = own(y) + own(y + 1)
                        update(y, both)
                        update(y + 1, both)
                    elif y % NP != 0:
                        update(y, own(y))

    @pl.loop(0, CHUNKS)
    def _(chunk):
        load(chunk).wait()
        prepare(chunk)
        apply_and_send(0, chunk)

    for stage in (1, 2):

        @pl.loop(0, CHUNKS)
        def _(chunk):
            finish(stage - 1, chunk)
            apply_and_send(stage, chunk)

    @pl.loop(0, CHUNKS)
    def _(chunk):
        finish(2, chunk)
        store(chunk).start()

    @pl.loop(0, 3 * CHUNKS)
    def _(step):
        for copy in copies(step):
            copy.wait_send()

    for chunk in range(CHUNKS):
        store(chunk).wait()


def physics_kernel(
    devices,
    final_hbm,
    inputs_ref,
    w_in,
    w_mid,
    w_top,
    w_out,
    bias_ref,
    span_ref,
    copied_hbm,
    tend_ref,
    parts_ref,
    outs,
    heat,
    spans,
    staged,
    copy_sem,
):
    pairs, _, width = inputs_ref.shape
    breadth = width // 2
    height = 2 * pairs
    n_out = w_out.shape[0]
    fetch = pltpu.make_async_copy(final_hbm, staged, copy_sem.at[0])
    write = pltpu.make_async_copy(staged, copied_hbm, copy_sem.at[1])
    fetch.start()
    for pair in range(pairs):
        spans[pair : pair + 1, :] = span_ref[:, pair * width : (pair + 1) * width]

    def silu(value):
        half = 0.5 * value
        return (half + half * jnp.tanh(half)).astype(jnp.bfloat16)

    def columns(pair):
        hidden = inputs_ref[pair]
        for layer, weight in enumerate((w_in, w_mid, w_top)):
            hidden = silu(
                jnp.dot(weight[...], hidden, preferred_element_type=jnp.float32)
                + bias_ref[:, layer : layer + 1]
            )
        out = (
            jnp.dot(w_out[...], hidden, preferred_element_type=jnp.float32)
            + bias_ref[0:n_out, 3:4]
        )
        heat[pl.ds(pair, 1), :] = jnp.sum(out[:LEV], axis=0, keepdims=True)
        for side in range(2):
            outs[pl.ds(2 * pair + side, n_out, stride=height), :] = out[
                :, side * breadth : (side + 1) * breadth
            ]

    pl.loop(0, pairs // 2)(columns)
    fetch.wait()
    write.start()
    pl.loop(pairs // 2, pairs)(columns)

    step = 15 * height

    @pl.loop(0, n_out * height // step)
    def _(block):
        at = pl.ds(pl.multiple_of(block * step, step), step)
        tend_ref[at, :] = outs[at, :].astype(jnp.bfloat16)

    @pl.loop(0, devices)
    def _(span):
        part = jnp.where(spans[...] == span, heat[...], 0.0)
        line = jnp.sum(part, axis=0, keepdims=True)
        parts_ref[span] = line[:, :breadth] + line[:, breadth:]

    write.wait()


def totals_kernel(n_face, n_elem, columns, parts_ref, out_ref, held, send_sem, recv_sem):
    devices = n_face * n_elem
    me = lax.axis_index("face") * n_elem + lax.axis_index("elem")
    barrier = pltpu.get_barrier_semaphore()

    def place(number):
        return (number // n_elem, number % n_elem)

    def copy(step):
        target = lax.rem(me + step, devices)
        return pltpu.make_async_remote_copy(
            src_ref=parts_ref.at[target],
            dst_ref=held.at[step],
            send_sem=send_sem.at[step],
            recv_sem=recv_sem.at[step],
            device_id=place(target),
            device_id_type=MESH,
        )

    @pl.loop(1, devices)
    def _(step):
        pl.semaphore_signal(
            barrier, inc=1, device_id=place(lax.rem(me + step, devices)), device_id_type=MESH
        )

    pl.semaphore_wait(barrier, devices - 1)

    @pl.loop(1, devices)
    def _(step):
        copy(step).start()

    held[0] = parts_ref[me]

    @pl.loop(1, devices)
    def _(step):
        copy(step).wait_recv()

    out_ref[0] = jnp.sum(held[...]) / columns

    @pl.loop(1, devices)
    def _(step):
        copy(step).wait_send()


def local(tables, state, speed_x, speed_y, w_in, b_in, w_mid, b_mid, w_top, b_top, w_out, b_out, span_of):
    feats, height, breadth = state.shape
    n_face, n_elem = lax.axis_size("face"), lax.axis_size("elem")
    devices = n_face * n_elem
    size = feats // CHUNKS
    steps = 3 * CHUNKS
    vmem = pl.BlockSpec(memory_space=pltpu.VMEM)
    hbm = pl.BlockSpec(memory_space=pl.ANY)
    n_out, hidden = w_out.shape

    final, inputs = pl.pallas_call(
        functools.partial(advect_kernel, n_face, n_elem, height, breadth),
        out_shape=(
            jax.ShapeDtypeStruct((feats * height, breadth), jnp.float32),
            jax.ShapeDtypeStruct((height // 2, feats, 2 * breadth), jnp.bfloat16),
        ),
        in_specs=[hbm, vmem, vmem, vmem, vmem],
        out_specs=(hbm, vmem),
        scratch_shapes=[
            pltpu.VMEM((feats * height, breadth), jnp.float32),
            pltpu.VMEM((height, feats, breadth), jnp.float32),
            pltpu.VMEM((height // NP * size, 8 * breadth), jnp.bfloat16),
            pltpu.VMEM((CHUNKS, 2, height // NP * size, 2 * breadth), jnp.float32),
            pltpu.VMEM((height // NP * size, NP * breadth), jnp.bfloat16),
            pltpu.VMEM((height // NP * size, NP * breadth), jnp.float32),
            pltpu.VMEM((steps, 2, size // 3, breadth), jnp.bfloat16),
            pltpu.VMEM((steps, 4, size // 3, breadth), jnp.bfloat16),
            pltpu.VMEM((steps, 2, size, breadth), jnp.bfloat16),
            pltpu.VMEM((steps, 2, size, breadth), jnp.bfloat16),
            pltpu.SemaphoreType.DMA((CHUNKS,)),
            pltpu.SemaphoreType.DMA((CHUNKS,)),
            pltpu.SemaphoreType.DMA((steps, 5)),
            pltpu.SemaphoreType.DMA((steps, 5)),
        ],
        compiler_params=pltpu.CompilerParams(
            collective_id=0, has_side_effects=True, vmem_limit_bytes=60 * 2**20
        ),
        name="advect",
    )(state.reshape(feats * height, breadth), jnp.stack([speed_x, speed_y], axis=1), *tables)

    bias = jnp.stack([b_in, b_mid, b_top, jnp.pad(b_out, (0, hidden - n_out))], axis=1)
    final, tend, parts = pl.pallas_call(
        functools.partial(physics_kernel, devices),
        out_shape=(
            jax.ShapeDtypeStruct((feats * height, breadth), jnp.float32),
            jax.ShapeDtypeStruct((n_out * height, breadth), jnp.bfloat16),
            jax.ShapeDtypeStruct((devices, 1, breadth), jnp.float32),
        ),
        in_specs=[hbm] + [vmem] * 7,
        out_specs=(hbm, vmem, vmem),
        scratch_shapes=[
            pltpu.VMEM((n_out * height, breadth), jnp.float32),
            pltpu.VMEM((height // 2, 2 * breadth), jnp.float32),
            pltpu.VMEM((height // 2, 2 * breadth), jnp.int32),
            pltpu.VMEM((feats * height, breadth), jnp.float32),
            pltpu.SemaphoreType.DMA((2,)),
        ],
        compiler_params=pltpu.CompilerParams(vmem_limit_bytes=60 * 2**20),
        name="physics",
    )(
        final,
        inputs,
        w_in,
        w_mid,
        w_top,
        w_out,
        bias,
        span_of.reshape(1, height * breadth),
    )
    span_heating = pl.pallas_call(
        functools.partial(totals_kernel, n_face, n_elem, height * breadth),
        out_shape=jax.ShapeDtypeStruct((1,), jnp.float32),
        in_specs=[vmem],
        out_specs=pl.BlockSpec(memory_space=pltpu.SMEM),
        scratch_shapes=[
            pltpu.VMEM((devices, 1, breadth), jnp.float32),
            pltpu.SemaphoreType.DMA((devices,)),
            pltpu.SemaphoreType.DMA((devices,)),
        ],
        compiler_params=pltpu.CompilerParams(collective_id=1, has_side_effects=True),
        name="totals",
    )(parts)
    return (
        final.reshape(state.shape),
        tend.reshape(n_out, height, breadth),
        span_heating,
    )


def solution(mesh):
    specs = (
        (P(None, "face", "elem"),) + (P(),) * 10 + (P("face", "elem", None, None),)
    )
    inner = jax.shard_map(
        local,
        mesh=mesh,
        in_specs=((P(), P(), P()),) + specs,
        out_specs=(P(None, "face", "elem"), P(None, "face", "elem"), P(("face", "elem"))),
        check_vma=False,
    )

    def whole(state, *rest):
        breadth = state.shape[2] // mesh.shape["elem"]
        made = (operator_tables(breadth),) + edge_tables(breadth)
        tables = tuple(jnp.asarray(table, dtype=jnp.bfloat16) for table in made)
        return inner(tables, state, *rest)

    return whole
```

profile of v0, /device:TPU:0, one launch (start us, length us, event | category | flops | bytes accessed | tf_op | source)
XLA Modules:
  0.0 67.8 jit_solution(3636497342990846378)
XLA Ops:
  0.6 0.7 %pad.4 = f32[512]{0:T(512)S(1)} pad(f32[360]{0:T(512)} %param.25, f32[]{:T(128)} %constant.8.clone.1), padding=0_152 | pad | bytes 3492 | tf_op jit(solution)/shard_map/jit(_pad)/pad | solution.py:495
  1.3 0.7 %pad_maximum_fusion.1 = f32[432,2]{0,1:T(2,128)S(1)} fusion(f32[432,1]{0,1:T(1,128)} %bitcast.13, f32[432,1]{0,1:T(1,128)} %bitcast.14), kind=kLoop, calls=%fused_computation.1 | loop fusion | flops 864 | bytes 6912 | tf_op jit(solution)/shard_map/stack | solution.py:493
  2.0 0.7 %pad_maximum_fusion = f32[512,4]{0,1:T(4,128)S(1)} fusion(f32[512,1]{0,1:T(1,128)S(1)} %bitcast.12, f32[512,1]{0,1:T(1,128)} %bitcast.15, f32[512,1]{0,1:T(1,128)} %bitcast.16, f32[512,1]{0,1:T(1,128)} %bitcast.17), kind=kLoop, calls=%fused_computation | loop fusion | flops 6144 | bytes 16384 | tf_op jit(solution)/shard_map/stack | solution.py:495
  2.8 0.8 %copy.26.speed_ref = f32[432,2]{1,0:T(8,128)} copy(f32[432,2]{0,1:T(2,128)S(1)} %pad_maximum_fusion.1) | data formatting | bytes 6912 | tf_op jit(solution)/shard_map/stack | solution.py:493
  3.6 0.9 %copy.28.bias_ref = f32[512,4]{1,0:T(8,128)} copy(f32[512,4]{0,1:T(4,128)S(1)} %pad_maximum_fusion) | data formatting | bytes 16384 | tf_op jit(solution)/shard_map/stack | solution.py:495
  4.4 2.0 %copy.27.w_in = bf16[512,432]{1,0:T(8,128)(2,1)} copy(bf16[512,432]{0,1:T(8,128)(2,1)} %param.18) | data formatting | bytes 884736 | tf_op args[3]
  6.5 35.0 %advect.1 = (f32[6912,128]{1,0:T(8,128)}, bf16[8,432,256]{2,1,0:T(8,128)(2,1)}) custom-call(f32[6912,128]{1,0:T(8,128)} %bitcast.10, f32[432,2]{1,0:T(8,128)} %copy.26.speed_ref, bf16[2,768,256]{2,1,0:T(8,128)(2,1)} %constant.9.clone.table_ref, bf16[512,256]{1,0:T(8,128)(2,1)} %constant.10.clone.pick_ref, bf16[128,512]{1,0:T(8,128)(2,1)} %constant.11.clone.place_ref), custom_call_target="tpu_custom_call" | custom-call | tf_op jit(solution)/shard_map/advect/pallas_call | solution.py:465
  41.5 15.0 %physics.1 = (f32[6912,128]{1,0:T(8,128)}, bf16[5760,128]{1,0:T(8,128)(2,1)}, f32[32,1,128]{2,1,0:T(1,128)}) custom-call(f32[6912,128]{1,0:T(8,128)} %get-tuple-element.8.final_hbm, bf16[8,432,256]{2,1,0:T(8,128)(2,1)} %get-tuple-element.9.inputs_ref, bf16[512,432]{1,0:T(8,128)(2,1)} %copy.27.w_in, bf16[512,512]{1,0:T(8,128)(2,1)} %w_mid.1, ...), custom_call_target="tpu_custom_call" | custom-call | tf_op jit(solution)/shard_map/physics/pallas_call | solution.py:496
  56.5 9.5 %totals.1 = f32[1]{0:T(128)} custom-call(f32[32,1,128]{2,1,0:T(1,128)} %get-tuple-element.12.parts_ref), custom_call_target="tpu_custom_call" | custom-call | tf_op jit(solution)/shard_map/totals/pallas_call | solution.py:524
where the time goes:
time: 68.1 us; the launch traced here: 67.8 us
  Pallas kernels  59.5 us (87%)
  local copies, waits for them, and re-layouts  4.4 us (6%)
  between operations  2.42 us (4%)
  other arithmetic  1.43 us (2%)
    pallas_call x1, Pallas kernels, local(): pl.pallas_call(functools.partial(advect_kernel, n_face, n_elem, height, b...  35 us
    pallas_call x1, Pallas kernels, local(): pl.pallas_call(functools.partial(physics_kernel, devices), out_shape=(jax...  15 us
    pallas_call x1, Pallas kernels, local(): pl.pallas_call(functools.partial(totals_kernel, n_face, n_elem, height *...  9.48 us
    unnamed x1, local copies, waits for them, and re-layouts  2.03 us

commit v1 on v0

--- a/solution.py
+++ b/solution.py
@@ -77,13 +77,21 @@
     return pick, place
 
 
+def to_columns(sources, lines, columns):
+    lines[...] = jnp.zeros_like(lines)
+    for at, source in enumerate(sources):
+        lines[at : at + 1, 0 : source.shape[1]] = source[...]
+    columns[...] = lines[...].T
+
+
 def advect_kernel(
     n_face,
     n_elem,
     height,
     breadth,
     state_hbm,
-    speed_ref,
+    speed_x,
+    speed_y,
     table_ref,
     pick_ref,
     place_ref,
@@ -95,6 +103,8 @@
     raw,
     rows16,
     edged,
+    lines,
+    speed_ref,
     x_send,
     x_recv,
     y_send,
@@ -104,7 +114,7 @@
     send_sem,
     recv_sem,
 ):
-    feats = speed_ref.shape[0]
+    feats = speed_x.shape[1]
     size = feats // CHUNKS
     rows = size * height
     elements = height // NP
@@ -124,6 +134,7 @@
     for chunk in range(CHUNKS):
         load(chunk).start()
 
+    to_columns((speed_x, speed_y), lines, speed_ref)
     barrier = pltpu.get_barrier_semaphore()
     for partner in partners:
         pl.semaphore_signal(barrier, inc=1, device_id=partner, device_id_type=MESH)
@@ -345,7 +356,10 @@
     w_mid,
     w_top,
     w_out,
-    bias_ref,
+    b_in,
+    b_mid,
+    b_top,
+    b_out,
     span_ref,
     copied_hbm,
     tend_ref,
@@ -354,6 +368,8 @@
     heat,
     spans,
     staged,
+    lines,
+    bias_ref,
     copy_sem,
 ):
     pairs, _, width = inputs_ref.shape
@@ -363,6 +379,7 @@
     fetch = pltpu.make_async_copy(final_hbm, staged, copy_sem.at[0])
     write = pltpu.make_async_copy(staged, copied_hbm, copy_sem.at[1])
     fetch.start()
+    to_columns((b_in, b_mid, b_top, b_out), lines, bias_ref)
     for pair in range(pairs):
         spans[pair : pair + 1, :] = span_ref[:, pair * width : (pair + 1) * width]
 
@@ -468,7 +485,7 @@
             jax.ShapeDtypeStruct((feats * height, breadth), jnp.float32),
             jax.ShapeDtypeStruct((height // 2, feats, 2 * breadth), jnp.bfloat16),
         ),
-        in_specs=[hbm, vmem, vmem, vmem, vmem],
+        in_specs=[hbm] + [vmem] * 5,
         out_specs=(hbm, vmem),
         scratch_shapes=[
             pltpu.VMEM((feats * height, breadth), jnp.float32),
@@ -477,6 +494,8 @@
             pltpu.VMEM((CHUNKS, 2, height // NP * size, 2 * breadth), jnp.float32),
             pltpu.VMEM((height // NP * size, NP * breadth), jnp.bfloat16),
             pltpu.VMEM((height // NP * size, NP * breadth), jnp.float32),
+            pltpu.VMEM((8, hidden), jnp.float32),
+            pltpu.VMEM((hidden, 8), jnp.float32),
             pltpu.VMEM((steps, 2, size // 3, breadth), jnp.bfloat16),
             pltpu.VMEM((steps, 4, size // 3, breadth), jnp.bfloat16),
             pltpu.VMEM((steps, 2, size, breadth), jnp.bfloat16),
@@ -490,9 +509,8 @@
             collective_id=0, has_side_effects=True, vmem_limit_bytes=60 * 2**20
         ),
         name="advect",
-    )(state.reshape(feats * height, breadth), jnp.stack([speed_x, speed_y], axis=1), *tables)
-
-    bias = jnp.stack([b_in, b_mid, b_top, jnp.pad(b_out, (0, hidden - n_out))], axis=1)
+    )(state.reshape(feats * height, breadth), speed_x[None], speed_y[None], *tables)
+
     final, tend, parts = pl.pallas_call(
         functools.partial(physics_kernel, devices),
         out_shape=(
@@ -500,13 +518,15 @@
             jax.ShapeDtypeStruct((n_out * height, breadth), jnp.bfloat16),
             jax.ShapeDtypeStruct((devices, 1, breadth), jnp.float32),
         ),
-        in_specs=[hbm] + [vmem] * 7,
+        in_specs=[hbm] + [vmem] * 10,
         out_specs=(hbm, vmem, vmem),
         scratch_shapes=[
             pltpu.VMEM((n_out * height, breadth), jnp.float32),
             pltpu.VMEM((height // 2, 2 * breadth), jnp.float32),
             pltpu.VMEM((height // 2, 2 * breadth), jnp.int32),
             pltpu.VMEM((feats * height, breadth), jnp.float32),
+            pltpu.VMEM((8, hidden), jnp.float32),
+            pltpu.VMEM((hidden, 8), jnp.float32),
             pltpu.SemaphoreType.DMA((2,)),
         ],
         compiler_params=pltpu.CompilerParams(vmem_limit_bytes=60 * 2**20),
@@ -518,7 +538,10 @@
         w_mid,
         w_top,
         w_out,
-        bias,
+        b_in[None],
+        b_mid[None],
+        b_top[None],
+        b_out[None],
         span_of.reshape(1, height * breadth),
     )
     span_heating = pl.pallas_call(

time: 68.1 us -> 65.7 us (0.965)
  other arithmetic: 1.43 us -> 0 us
  local copies, waits for them, and re-layouts: 4.4 us -> 3.3 us
    another operation x2 -> x0, local copies, waits for them, and re-layouts: 1.69 us -> none  [the longest x1 0.85 us: local(): jnp.stack([b_in, b_mid, b_top, jnp.pad(b_out, (0, hidden - n_out))], axis=1)]
    another operation x2 -> x0, other arithmetic: 1.43 us -> none  [the longest x1 0.73 us: local(): jnp.stack([b_in, b_mid, b_top, jnp.pad(b_out, (0, hidden - n_out))], axis=1)]
    broadcast_in_dim x0 -> x1, local copies, waits for them, and re-layouts: none -> 1.27 us  [local(): b_out[None]]
    pad x1 -> x0, local copies, waits for them, and re-layouts: 0.69 us -> none  [local(): jnp.pad(b_out, (0, hidden - n_out))]
where the time goes in v1:
time: 65.7 us; the launch traced here: 65.5 us
  Pallas kernels  59.7 us (91%)
  local copies, waits for them, and re-layouts  3.3 us (5%)
  between operations  2.41 us (4%)
    pallas_call x1, Pallas kernels, local(): pl.pallas_call(functools.partial(advect_kernel, n_face, n_elem, height, b...  35.2 us
    pallas_call x1, Pallas kernels, local(): pl.pallas_call(functools.partial(physics_kernel, devices), out_shape=(jax...  15.1 us
    pallas_call x1, Pallas kernels, local(): pl.pallas_call(functools.partial(totals_kernel, n_face, n_elem, height *...  9.48 us
    unnamed x1, local copies, waits for them, and re-layouts  2.03 us

profile of v1, /device:TPU:0, one launch (start us, length us, event | category | flops | bytes accessed | tf_op | source)
XLA Modules:
  0.0 65.5 jit_solution(1652539461987438525)
XLA Ops:
  0.6 1.3 %broadcast_in_dim.23.b_out = f32[1,360]{1,0:T(1,128)} reshape(f32[360]{0:T(512)} %param.25) | data formatting | bytes 2880 | tf_op jit(solution)/shard_map/broadcast_in_dim | solution.py:544
  1.9 2.0 %copy.18.w_in = bf16[512,432]{1,0:T(8,128)(2,1)} copy(bf16[512,432]{0,1:T(8,128)(2,1)} %param.18) | data formatting | bytes 884736 | tf_op args[3]
  3.9 35.2 %advect.1 = (f32[6912,128]{1,0:T(8,128)}, bf16[8,432,256]{2,1,0:T(8,128)(2,1)}) custom-call(f32[6912,128]{1,0:T(8,128)} %bitcast.9, f32[1,432]{1,0:T(1,128)} %bitcast.11, f32[1,432]{1,0:T(1,128)} %bitcast.12, bf16[2,768,256]{2,1,0:T(8,128)(2,1)} %constant.6.clone.table_ref, bf16[512,256]{1,0:T(8,128)(2,1)} %constant.7.clone.pick_ref, ...), custom_call_target="tpu_custom_call" | custom-call | tf_op jit(solution)/shard_map/advect/pallas_call | solution.py:482
  39.1 15.1 %physics.1 = (f32[6912,128]{1,0:T(8,128)}, bf16[5760,128]{1,0:T(8,128)(2,1)}, f32[32,1,128]{2,1,0:T(1,128)}) custom-call(f32[6912,128]{1,0:T(8,128)} %get-tuple-element.8.final_hbm, bf16[8,432,256]{2,1,0:T(8,128)(2,1)} %get-tuple-element.9.inputs_ref, bf16[512,432]{1,0:T(8,128)(2,1)} %copy.18.w_in, bf16[512,512]{1,0:T(8,128)(2,1)} %w_mid.1, ...), custom_call_target="tpu_custom_call" | custom-call | tf_op jit(solution)/shard_map/physics/pallas_call | solution.py:514
  54.2 9.5 %totals.1 = f32[1]{0:T(128)} custom-call(f32[32,1,128]{2,1,0:T(1,128)} %get-tuple-element.12.parts_ref), custom_call_target="tpu_custom_call" | custom-call | tf_op jit(solution)/shard_map/totals/pallas_call | solution.py:547
